TPU v7x, 32 devices: a whole 2x2x4 slice. The times are simulated.
32 devices in a mesh: groups: 2 (over y), seq: 8 (over z, x), head: 2 (over core).
Axes of the slice: x: 2, y: 2, z: 4, core: 2. Of those that a mesh axis runs over, the one named last changes fastest.
Arguments:
- text_query_rows: bfloat16 [2048, 8192], P(('groups', 'seq'), 'head'), parts along dimension 0, may hold values from -40 to 40, as said below
- text_key_value: bfloat16 [2, 2048, 1024], P(None, ('groups', 'seq'), 'head'), parts along dimension 1, may hold values from -4 to 4, as said below
- doc_ids: int32 [2048], P(('groups', 'seq')), parts along dimension 0, may hold values from 0 to 3, never falling along the last dimension, each value on 1 to 512 neighbouring positions
- tile_span: int32 [2048, 2], P(('groups', 'seq')), parts along dimension 0, may hold values from 0 to 8, as said below
- vision_hidden: bfloat16 [4096, 1280], P(('groups', 'seq')), parts along dimension 0, may hold values from -6 to 6
- vision_qkv: bfloat16 [3, 4096, 1280], P(None, ('groups', 'seq'), 'head'), parts along dimension 1, may hold values from -6 to 6, as said below
- vision_out_weight: bfloat16 [1280, 1280], P('head'), may hold values from -0.625 to 0.625
- cross_keyvalue_weight: bfloat16 [1280, 2, 1024], P('seq', None, 'head'), may hold values from -0.15625 to 0.15625
- cross_gate: float32 [64], P('head'), may hold values from -1.5 to 1.5
Outputs:
- attention_out: bfloat16 [2048, 8192], P(('groups', 'seq'), 'head'), parts along dimension 0
There are 2 independent parts, one for each index of `groups`. A program takes and returns all parts, laid end to end along the dimension named above; an argument that names none is the same for every part. Nothing has to cross between parts.
Inputs may be any that keep to these rules, and one draw needn't show every extreme that they name: `tile_span`: each text token's span is an interval of the tiles of its own block b = p // 128 and of block b - 1 (first <= second, both between b - 1 and b + 1, never below 0); it may be empty. `doc_ids`: never falling along the document; each segment holds 1 to 512 tokens. `text_query_rows`: real values. `text_key_value`: real values. `vision_qkv`: real values.
All inputs are finite; a program needn't handle non-finite values.
Results may differ from a plain program's by a relative error of at most 0.024.
Values may be sent and summed in bfloat16 or wider, within the bound.
A program may use at most 64 MiB of HBM per device.

v0:
```python
import math
import jax
import jax.numpy as jnp
from jax import lax
from jax.sharding import PartitionSpec as P

HEAD_SIZE = 128
VHD = 80
WINDOW_BLOCKS = 2


def passed_along(block, axis, distance):
    devices = range(lax.axis_size(axis))
    route = [(i - distance, i) for i in devices if i - distance in devices]
    return lax.ppermute(block, axis, route)


def attend_heads(query_rows, keys, allowed_mask):
    scores = jnp.einsum(
        "tgrd,kgd->grtk", query_rows, keys, preferred_element_type=jnp.float32
    ) / math.sqrt(HEAD_SIZE)
    scores = jnp.where(allowed_mask[None, None], scores, -1e30)
    return jax.nn.softmax(scores, axis=-1)


def per_device(
    text_query_rows,
    text_key_value,
    doc_ids,
    tile_span,
    vision_hidden,
    vision_qkv,
    vision_out_weight,
    cross_keyvalue_weight,
    cross_gate,
):
    text_rows = text_query_rows.shape[0]
    tile_rows = vision_hidden.shape[0]
    kv_cols = text_key_value.shape[2]
    kv_heads = kv_cols // HEAD_SIZE
    query_group_ratio = text_query_rows.shape[1] // HEAD_SIZE // kv_heads
    seq_index = lax.axis_index("seq")
    vision_query = vision_qkv[0].reshape(tile_rows, -1, VHD)
    vision_key = vision_qkv[1].reshape(tile_rows, -1, VHD)
    vision_value = vision_qkv[2].reshape(tile_rows, -1, VHD)
    vision_scores = jnp.einsum(
        "qhd,khd->hqk", vision_query, vision_key, preferred_element_type=jnp.float32
    ) / math.sqrt(VHD)
    vision_weights = jax.nn.softmax(vision_scores, axis=-1).astype(jnp.bfloat16)
    vision_attn = jnp.einsum(
        "hqk,khd->qhd", vision_weights, vision_value, preferred_element_type=jnp.float32
    )
    vision_attn = vision_attn.astype(jnp.bfloat16).reshape(tile_rows, -1)
    partial_mix = jnp.dot(vision_attn, vision_out_weight, preferred_element_type=jnp.float32)
    mixed_sum = lax.psum(partial_mix, "head") + vision_hidden.astype(jnp.float32)
    image_norm = (
        mixed_sum * lax.rsqrt(jnp.mean(mixed_sum * mixed_sum, axis=-1, keepdims=True) + 1e-05)
    ).astype(jnp.bfloat16)
    image_key_value = jnp.einsum(
        "ic,cjf->ijf",
        image_norm,
        lax.all_gather(cross_keyvalue_weight, "seq", axis=0, tiled=True),
        preferred_element_type=jnp.float32,
    ).astype(jnp.bfloat16)
    earlier_tile = passed_along(image_key_value, "seq", 1)
    blocks = [(text_key_value, doc_ids)]
    current_kv, current_docs = (text_key_value, doc_ids)
    for repeat_count in range(WINDOW_BLOCKS):
        current_kv, current_docs = passed_along((current_kv, current_docs), "seq", 1)
        blocks.insert(0, (current_kv, current_docs))
    all_keyval = jnp.concatenate([member[0] for member in blocks], axis=1)
    all_docs = jnp.concatenate([member[1] for member in blocks], axis=0)
    key_pos = (seq_index - WINDOW_BLOCKS) * text_rows + jnp.arange(
        (WINDOW_BLOCKS + 1) * text_rows, dtype=jnp.int32
    )
    query_pos = seq_index * text_rows + jnp.arange(text_rows, dtype=jnp.int32)
    allowed_mask = (
        (all_docs[None, :] == doc_ids[:, None])
        & (key_pos[None, :] <= query_pos[:, None])
        & (key_pos[None, :] >= 0)
    )
    query_rows = text_query_rows.reshape(text_rows, kv_heads, query_group_ratio, HEAD_SIZE)
    self_attention_weights = attend_heads(
        query_rows, all_keyval[0].reshape(-1, kv_heads, HEAD_SIZE), allowed_mask
    ).astype(jnp.bfloat16)
    self_output = jnp.einsum(
        "ycmq,qyb->mycb",
        self_attention_weights,
        all_keyval[1].reshape(-1, kv_heads, HEAD_SIZE),
        preferred_element_type=jnp.float32,
    )
    self_output = self_output.reshape(text_rows, -1)
    image_all = jnp.concatenate([earlier_tile, image_key_value], axis=0)
    tile_ids = seq_index - 1 + jnp.arange(2 * tile_rows, dtype=jnp.int32) // tile_rows
    low_tile = tile_span[:, 0]
    high_tile = tile_span[:, 1]
    visible_mask = (tile_ids[None, :] >= low_tile[:, None]) & (
        tile_ids[None, :] < high_tile[:, None]
    )
    image_present = (high_tile > low_tile).astype(jnp.float32)
    cross_probabilities = (
        attend_heads(query_rows, image_all[:, 0].reshape(-1, kv_heads, HEAD_SIZE), visible_mask)
        * image_present[None, None, :, None]
    )
    cross_probabilities = cross_probabilities.astype(jnp.bfloat16)
    cross_output = jnp.einsum(
        "ycmq,qyb->mycb",
        cross_probabilities,
        image_all[:, 1].reshape(-1, kv_heads, HEAD_SIZE),
        preferred_element_type=jnp.float32,
    )
    cross_output = cross_output.reshape(text_rows, -1)
    gate_cols = jnp.repeat(jnp.tanh(cross_gate), HEAD_SIZE)
    return (self_output + gate_cols[None, :] * cross_output).astype(jnp.bfloat16)


def solution(mesh):
    placed = (
        P(("groups", "seq"), "head"),
        P(None, ("groups", "seq"), "head"),
        P(("groups", "seq")),
        P(("groups", "seq"), None),
        P(("groups", "seq"), None),
        P(None, ("groups", "seq"), "head"),
        P("head", None),
        P("seq", None, "head"),
        P("head"),
    )
    return jax.shard_map(
        per_device,
        mesh=mesh,
        in_specs=placed,
        out_specs=P(("groups", "seq"), "head"),
        check_vma=False,
    )
```

profile of v0, /device:TPU:8, one launch (start us, length us, event | category | flops | bytes accessed | tf_op | source)
XLA Modules:
  0.0 130.6 jit_solution(16018390959418832903)
XLA Ops:
  9.3 2.2 %fusion.38 = (f32[8,256]{1,0:T(8,128)S(1)}, f32[8,256,256]{1,2,0:T(8,128)}) fusion(bf16[256,8,80]{0,2,1:T(8,128)(2,1)S(1)} %bitcast.88, bf16[256,8,80]{0,2,1:T(8,128)(2,1)S(1)} %bitcast.87), kind=kOutput, calls=%fused_computation.70 | convolution fusion | flops 85459200 | bytes 2760704 | tf_op jit(solution)/shard_map/sub | solution.py:49
  11.5 1.9 %convolution_convert_fusion.1 = bf16[8,256,80]{1,2,0:T(8,128)(2,1)S(1)} fusion(bf16[256,8,80]{0,2,1:T(8,128)(2,1)S(1)} %bitcast.89, f32[8,256,256]{1,2,0:T(8,128)} %get-tuple-element.17, f32[8,256]{1,0:T(8,128)S(1)} %get-tuple-element.16), kind=kOutput, calls=%fused_computation.28 | convolution fusion | flops 85098496 | bytes 2760704 | tf_op jit(solution)/shard_map/hqk,khd->qhd/dot_general | solution.py:50
  13.4 1.8 %fusion.40 = f32[256,1280]{1,0:T(8,128)} fusion(bf16[256,640]{0,1:T(8,128)(2,1)S(1)} %bitcast.86, bf16[640,1280]{1,0:T(8,128)(2,1)S(1)} %copy-done), kind=kOutput, calls=%fused_computation.72 | convolution fusion | flops 419430400 | bytes 3276800 | tf_op jit(solution)/shard_map/dot_general | solution.py:54
  16.1 3.4 %collective-permute-start.2 = (s32[128]{0:T(128)S(1)}, s32[128]{0:T(128)S(1)}, u32[]{:S(2)}, u32[]{:S(2)}) collective-permute-start(s32[128]{0:T(128)S(1)} %copy-done.5), channel_id=1, source_target_pairs={{0,2},{2,4},{4,6},{6,8},{8,10},{10,12},{12,14},{1,3},{3,5},{5,7},{... | collective-permute-start | bytes 1544 | tf_op jit(solution)/shard_map/ppermute | solution.py:15
  19.7 3.5 %collective-permute-start = (bf16[2,128,512]{1,2,0:T(8,128)(2,1)S(1)}, bf16[2,128,512]{1,2,0:T(8,128)(2,1)S(1)}, u32[]{:S(2)}, u32[]{:S(2)}) collective-permute-start(bf16[2,128,512]{1,2,0:T(8,128)(2,1)S(1)} %copy.24), channel_id=1, source_target_pairs={{0,2},{2,4},{4,6},{6,8},{8,10},{10,12},{12,14},{1,3},{3,5},{5,7},{... | collective-permute-start | bytes 786440 | tf_op jit(solution)/shard_map/ppermute | solution.py:15
  23.5 3.4 %collective-permute-start.3 = (s32[128]{0:T(128)S(1)}, s32[128]{0:T(128)S(1)}, u32[]{:S(2)}, u32[]{:S(2)}) collective-permute-start(s32[128]{0:T(128)S(1)} %collective-permute-done.2), channel_id=1, source_target_pairs={{0,2},{2,4},{4,6},{6,8},{8,10},{10,12},{12,14},{1,3},{3,5},{5,7},{... | collective-permute-start | bytes 1544 | tf_op jit(solution)/shard_map/ppermute | solution.py:15
  26.9 1.5 %copy.52 = bf16[16,8,32,128]{3,2,1,0:T(8,128)(2,1)S(1)} copy(bf16[16,8,32,128]{3,1,2,0:T(8,128)(2,1)} %bitcast.83) | data formatting | bytes 2097152
  28.4 2.6 %collective-permute-done = bf16[2,128,512]{1,2,0:T(8,128)(2,1)S(1)} collective-permute-done((bf16[2,128,512]{1,2,0:T(8,128)(2,1)S(1)}, bf16[2,128,512]{1,2,0:T(8,128)(2,1)S(1)}, u32[]{:S(2)}, u32[]{:S(2)}) %collective-permute-start) | collective-permute-done | bytes 262176 | tf_op jit(solution)/shard_map/ppermute | solution.py:15
  30.9 3.1 %collective-permute-start.1 = (bf16[2,128,512]{1,2,0:T(8,128)(2,1)S(1)}, bf16[2,128,512]{1,2,0:T(8,128)(2,1)S(1)}, u32[]{:S(2)}, u32[]{:S(2)}) collective-permute-start(bf16[2,128,512]{1,2,0:T(8,128)(2,1)S(1)} %collective-permute-done), channel_id=1, source_target_pairs={{0,2},{2,4},{4,6},{6,8},{8,10},{10,12},{12,14},{1,3},{3,5},{5,7},{... | collective-permute-start | bytes 786440 | tf_op jit(solution)/shard_map/ppermute | solution.py:15
  34.2 12.1 %collective-permute-done.1 = bf16[2,128,512]{1,2,0:T(8,128)(2,1)S(1)} collective-permute-done((bf16[2,128,512]{1,2,0:T(8,128)(2,1)S(1)}, bf16[2,128,512]{1,2,0:T(8,128)(2,1)S(1)}, u32[]{:S(2)}, u32[]{:S(2)}) %collective-permute-start.1) | collective-permute-done | bytes 262176 | tf_op jit(solution)/shard_map/ppermute | solution.py:15
  48.4 3.7 %fusion.37 = (f32[4,8,128]{2,1,0:T(8,128)S(1)}, f32[4,8,128,384]{2,3,1,0:T(8,128)}) fusion(f32[4,384,128,8]{2,1,3,0:T(8,128)S(1)} %fusion.17, pred[128,384]{0,1:T(8,128)(4,1)S(1)} %and_and_fusion), kind=kOutput, calls=%fused_computation.69 | output fusion | flops 9437567 | bytes 12648448 | tf_op jit(solution)/shard_map/sub | solution.py:23
  52.1 1.6 %multiply_reduce_fusion.1 = f32[256]{0:T(256)S(1)} fusion(f32[256,1280]{1,0:T(8,128)} %all-reduce.2.cloned.1.call-done, bf16[256,1280]{1,0:T(8,128)(2,1)S(1)} %copy-done.1), kind=kLoop, calls=%fused_computation.25 | loop fusion | flops 1310464 | bytes 1967104 | tf_op jit(solution)/shard_map/reduce_sum | solution.py:57
  53.7 23.4 %all-gather.2.cloned.1.call-done = bf16[1280,2,512]{2,0,1:T(8,128)(2,1)} async-done(((bf16[160,2,512]{2,0,1:T(8,128)(2,1)}), bf16[1280,2,512]{2,0,1:T(8,128)(2,1)}) %all-gather.2.cloned.1.call-update) | async-done | bytes 2621456 | tf_op jit(solution)/shard_map/all_gather | solution.py:62
  77.1 3.9 %convolution_convert_fusion = bf16[256,2,512]{2,0,1:T(8,128)(2,1)} fusion(bf16[1280,2,512]{2,0,1:T(8,128)(2,1)} %all-gather.2.cloned.1.call-done, f32[256,1280]{1,0:T(8,128)} %all-reduce.2.cloned.1.call-done, bf16[256,1280]{1,0:T(8,128)(2,1)S(1)} %copy-done.1, f32[256]{0:T(256)S(1)} %add_rsqrt_fusion), kind=kOutput, calls=%fused_computation.27 | convolution fusion | flops 672661504 | bytes 5112832 | tf_op jit(solution)/shard_map/ic,cjf->ijf/dot_general | solution.py:59
  81.0 2.6 %collective-permute-start.4 = (bf16[256,2,512]{2,0,1:T(8,128)(2,1)}, bf16[256,2,512]{2,0,1:T(8,128)(2,1)S(1)}, u32[]{:S(2)}, u32[]{:S(2)}) collective-permute-start(bf16[256,2,512]{2,0,1:T(8,128)(2,1)} %convolution_convert_fusion), channel_id=1, source_target_pairs={{0,2},{2,4},{4,6},{6,8},{8,10},{10,12},{12,14},{1,3},{3,5},{5,7},{... | collective-permute-start | bytes 1572872 | tf_op jit(solution)/shard_map/ppermute | solution.py:15
  83.6 4.9 %fusion.11 = f32[4,128,8,128]{3,1,2,0:T(8,128)} fusion(bf16[384,4,128,1]{0,2,3,1:T(8,128)(2,1)S(1)} %bitcast.85, f32[4,8,128,384]{2,3,1,0:T(8,128)} %get-tuple-element.15, f32[4,8,128]{2,1,0:T(8,128)S(1)} %get-tuple-element.14), kind=kOutput, calls=%fused_computation.17 | convolution fusion | flops 405798912 | bytes 8798208 | tf_op jit(solution)/shard_map/ycmq,qyb->mycb/dot_general | solution.py:86
  88.5 2.9 %copy.39 = f32[128,4096]{1,0:T(8,128)} copy(f32[128,4096]{0,1:T(8,128)} %bitcast.81) | data formatting | bytes 4194304 | tf_op jit(solution)/shard_map/reshape | solution.py:92
  91.5 5.0 %collective-permute-done.4 = bf16[256,2,512]{2,0,1:T(8,128)(2,1)S(1)} collective-permute-done((bf16[256,2,512]{2,0,1:T(8,128)(2,1)}, bf16[256,2,512]{2,0,1:T(8,128)(2,1)S(1)}, u32[]{:S(2)}, u32[]{:S(2)}) %collective-permute-start.4) | collective-permute-done | bytes 524320 | tf_op jit(solution)/shard_map/ppermute | solution.py:15
  96.5 2.1 %pad_maximum_fusion.1 = (bf16[512,1,512]{2,0,1:T(8,128)(2,1)}, bf16[512,1,512]{2,0,1:T(8,128)(2,1)}) fusion(bf16[256,2,512]{2,0,1:T(8,128)(2,1)} %convolution_convert_fusion, bf16[256,2,512]{2,0,1:T(8,128)(2,1)S(1)} %collective-permute-done.4), kind=kLoop, calls=%fused_computation.40 | loop fusion | flops 2097152 | bytes 2097152 | tf_op jit(solution)/shard_map/concatenate | solution.py:93
  99.8 4.5 %fusion.15 = f32[4,512,128,8]{2,1,3,0:T(8,128)} fusion(bf16[128,4,8,128]{3,2,1,0:T(8,128)(2,1)S(1)} %bitcast.78, bf16[512,4,128,1]{2,1,0,3:T(4,128)(2,1)S(1)} %bitcast.79), kind=kOutput, calls=%fused_computation.32 | convolution fusion | flops 536870912 | bytes 9961472 | tf_op jit(solution)/shard_map/tgrd,kgd->grtk/dot_general | solution.py:19
  105.5 8.9 %fusion.39 = (f32[4,8,128]{2,1,0:T(8,128)S(1)}, f32[4,8,128,512]{2,3,1,0:T(8,128)S(1)}) fusion(f32[4,512,128,8]{2,1,3,0:T(8,128)} %fusion.15, pred[128,512]{0,1:T(8,128)(4,1)S(1)} %compare_and_fusion), kind=kOutput, calls=%fused_computation.71 | output fusion | flops 12583423 | bytes 16859136 | tf_op jit(solution)/shard_map/sub | solution.py:23
  114.4 2.3 %fusion.8 = f32[4,128,8,128]{3,1,2,0:T(8,128)} fusion(bf16[512,4,128,1]{0,2,3,1:T(8,128)(2,1)S(1)} %bitcast.84, f32[4,8,128,512]{2,3,1,0:T(8,128)S(1)} %get-tuple-element.19, f32[128]{0:T(128)S(1)} %compare_convert_fusion, f32[4,8,128]{2,1,0:T(8,128)S(1)} %get-tuple-element.18), kind=kOutput, calls=%fused_computation.14 | convolution fusion | flops 543162368 | bytes 11026944 | tf_op jit(solution)/shard_map/ycmq,qyb->mycb/dot_general | solution.py:106
  116.8 2.9 %copy.38 = f32[128,4096]{1,0:T(8,128)} copy(f32[128,4096]{0,1:T(8,128)} %bitcast.80) | data formatting | bytes 4194304 | tf_op jit(solution)/shard_map/reshape | solution.py:112
  119.7 3.5 %add_convert_fusion = bf16[128,4096]{1,0:T(8,128)(2,1)} fusion(f32[128,4096]{1,0:T(8,128)} %copy.39, f32[128,4096]{1,0:T(8,128)} %copy.38, f32[4096]{0:T(1024)S(1)} %broadcast_bitcast_fusion), kind=kLoop, calls=%fused_computation.19 | loop fusion | flops 1572864 | bytes 5259264 | tf_op jit(solution)/shard_map/convert_element_type | solution.py:114
  (46 shorter events, 7.8 us)
Async XLA Ops:
  7.4 6.0 %copy-start = (bf16[640,1280]{1,0:T(8,128)(2,1)S(1)}, bf16[640,1280]{1,0:T(8,128)(2,1)}, u32[]{:S(2)}) copy-start(bf16[640,1280]{1,0:T(8,128)(2,1)} %param.15) | copy-start | bytes 4915204
  7.4 44.7 %all-reduce.2.cloned.1.call-start = ((), (), s32[]{:S(2)}) async-start(), calls=%async_computation | async-start | bytes 2621440 | tf_op jit(solution)/shard_map/psum | solution.py:55
  13.4 1.9 %copy-start.3 = (bf16[160,2,512]{2,1,0:T(2,128)(2,1)S(1)}, bf16[160,2,512]{2,1,0:T(2,128)(2,1)}, u32[]{:S(2)}) copy-start(bf16[160,2,512]{2,1,0:T(2,128)(2,1)} %param.16) | copy-start | bytes 983044
  13.4 2.7 %copy-start.5 = (s32[128]{0:T(128)S(1)}, s32[128]{0:T(128)}, u32[]{:S(2)}) copy-start(s32[128]{0:T(128)} %param.11) | copy-start | bytes 1540
  13.4 6.1 %copy-start.4 = (bf16[2,128,512]{2,1,0:T(8,128)(2,1)S(1)}, bf16[2,128,512]{2,1,0:T(8,128)(2,1)}, u32[]{:S(2)}) copy-start(bf16[2,128,512]{2,1,0:T(8,128)(2,1)} %param.10) | copy-start | bytes 786436
  13.4 9.7 %copy-start.7 = (f32[32]{0:T(128)S(1)}, f32[32]{0:T(128)}, u32[]{:S(2)}) copy-start(f32[32]{0:T(128)} %param.17) | copy-start | bytes 388
  13.4 9.8 %copy-start.6 = (s32[128,2]{0,1:T(2,128)S(1)}, s32[128,2]{0,1:T(2,128)}, u32[]{:S(2)}) copy-start(s32[128,2]{0,1:T(2,128)} %param.12) | copy-start | bytes 3076
  15.2 61.9 %all-gather.2.cloned.1.call-start = ((), (), s32[]{:S(2)}) async-start(), calls=%async_computation.1 | async-start | bytes 2949120 | tf_op jit(solution)/shard_map/all_gather | solution.py:62
  16.1 7.4 %collective-permute-start.2 = (s32[128]{0:T(128)S(1)}, s32[128]{0:T(128)S(1)}, u32[]{:S(2)}, u32[]{:S(2)}) collective-permute-start(s32[128]{0:T(128)S(1)} %copy-done.5), channel_id=1, source_target_pairs={{0,2},{2,4},{4,6},{6,8},{8,10},{10,12},{12,14},{1,3},{3,5},{5,7},{... | collective-permute-start | bytes 1544 | tf_op jit(solution)/shard_map/ppermute | solution.py:15
  19.7 11.3 %collective-permute-start = (bf16[2,128,512]{1,2,0:T(8,128)(2,1)S(1)}, bf16[2,128,512]{1,2,0:T(8,128)(2,1)S(1)}, u32[]{:S(2)}, u32[]{:S(2)}) collective-permute-start(bf16[2,128,512]{1,2,0:T(8,128)(2,1)S(1)} %copy.24), channel_id=1, source_target_pairs={{0,2},{2,4},{4,6},{6,8},{8,10},{10,12},{12,14},{1,3},{3,5},{5,7},{... | collective-permute-start | bytes 786440 | tf_op jit(solution)/shard_map/ppermute | solution.py:15
  23.5 10.5 %collective-permute-start.3 = (s32[128]{0:T(128)S(1)}, s32[128]{0:T(128)S(1)}, u32[]{:S(2)}, u32[]{:S(2)}) collective-permute-start(s32[128]{0:T(128)S(1)} %collective-permute-done.2), channel_id=1, source_target_pairs={{0,2},{2,4},{4,6},{6,8},{8,10},{10,12},{12,14},{1,3},{3,5},{5,7},{... | collective-permute-start | bytes 1544 | tf_op jit(solution)/shard_map/ppermute | solution.py:15
  30.9 15.5 %collective-permute-start.1 = (bf16[2,128,512]{1,2,0:T(8,128)(2,1)S(1)}, bf16[2,128,512]{1,2,0:T(8,128)(2,1)S(1)}, u32[]{:S(2)}, u32[]{:S(2)}) collective-permute-start(bf16[2,128,512]{1,2,0:T(8,128)(2,1)S(1)} %collective-permute-done), channel_id=1, source_target_pairs={{0,2},{2,4},{4,6},{6,8},{8,10},{10,12},{12,14},{1,3},{3,5},{5,7},{... | collective-permute-start | bytes 786440 | tf_op jit(solution)/shard_map/ppermute | solution.py:15
  48.4 3.7 %copy-start.1 = (bf16[256,1280]{1,0:T(8,128)(2,1)S(1)}, bf16[256,1280]{1,0:T(8,128)(2,1)}, u32[]{:S(2)}) copy-start(bf16[256,1280]{1,0:T(8,128)(2,1)} %param.13) | copy-start | bytes 1966084
  77.1 6.5 %copy-start.2 = (bf16[1,384,512]{1,2,0:T(8,128)(2,1)S(1)}, bf16[1,384,512]{1,2,0:T(8,128)(2,1)}, u32[]{:S(2)}) copy-start(bf16[1,384,512]{1,2,0:T(8,128)(2,1)} %get-tuple-element.11) | copy-start | bytes 1179652
  81.0 15.5 %collective-permute-start.4 = (bf16[256,2,512]{2,0,1:T(8,128)(2,1)}, bf16[256,2,512]{2,0,1:T(8,128)(2,1)S(1)}, u32[]{:S(2)}, u32[]{:S(2)}) collective-permute-start(bf16[256,2,512]{2,0,1:T(8,128)(2,1)} %convolution_convert_fusion), channel_id=1, source_target_pairs={{0,2},{2,4},{4,6},{6,8},{8,10},{10,12},{12,14},{1,3},{3,5},{5,7},{... | collective-permute-start | bytes 1572872 | tf_op jit(solution)/shard_map/ppermute | solution.py:15
Sparse Core Ops, SparseCore 0:
  15.3 21.4 all-reduce.1
Sparse Core Ops, SparseCore 1:
  17.9 59.1 all-gather.1
where the time goes:
time: 131 us
  waiting for transfers between devices  43.2 us (33%)
  matrix products  22.5 us (17%)
  other arithmetic  20.2 us (15%)
  starting transfers between devices  16 us (12%)
  between operations  15.1 us (12%)
  local copies, waits for them, and re-layouts  13.6 us (10%)
    all_gather x1, waiting for transfers between devices, per_device(): lax.all_gather(cross_keyvalue_weight, 'seq', axis=0, tiled=True)  23.4 us
    ppermute x5, waiting for transfers between devices, passed_along(): return lax.ppermute(block, axis, route)  19.7 us
    ppermute x5, starting transfers between devices, passed_along(): return lax.ppermute(block, axis, route)  16 us
    sub x2, other arithmetic, attend_heads(): return jax.nn.softmax(scores, axis=-1)  12.6 us
    dot_general x2, matrix products, attend_heads(): jnp.einsum('tgrd,kgd->grtk', query_rows, keys, preferred_element_type=jnp...  5.54 us
    dot_general x1, matrix products, per_device(): jnp.einsum('ycmq,qyb->mycb', self_attention_weights, all_keyval[1].reshap...  4.89 us
    dot_general x1, matrix products, per_device(): jnp.einsum('ic,cjf->ijf', image_norm, lax.all_gather(cross_keyvalue_weigh...  3.87 us
    convert_element_type x1, other arithmetic, per_device(): (self_output + gate_cols[None, :] * cross_output).astype(jnp.bfloat16)  3.46 us
  transfers between devices with their start and end apart: 7, of which 4 were waited for; matrix products, arithmetic and copies ran while one was open for 14% of the time, Pallas kernels for 0%

commit v1 on v0

--- a/solution.py
+++ b/solution.py
@@ -7,6 +7,18 @@
 HEAD_SIZE = 128
 VHD = 80
 WINDOW_BLOCKS = 2
+
+
+def doubled_up(x, axis, dim):
+    ways, here, turn = (lax.axis_size(axis), lax.axis_index(axis), x.shape[dim])
+    line, have = (x, 1)
+    while have < ways:
+        line = jnp.concatenate(
+            [line, lax.ppermute(line, axis, [(d, (d - have) % ways) for d in range(ways)])],
+            axis=dim,
+        )
+        have = 2 * have
+    return jnp.roll(line, here * turn, axis=dim)
 
 
 def passed_along(block, axis, distance):
@@ -59,7 +71,7 @@
     image_key_value = jnp.einsum(
         "ic,cjf->ijf",
         image_norm,
-        lax.all_gather(cross_keyvalue_weight, "seq", axis=0, tiled=True),
+        doubled_up(cross_keyvalue_weight, "seq", 0),
         preferred_element_type=jnp.float32,
     ).astype(jnp.bfloat16)
     earlier_tile = passed_along(image_key_value, "seq", 1)

time: 131 us -> 169 us (1.29)
  waiting for transfers between devices: 43.2 us -> 68.7 us
  local copies, waits for them, and re-layouts: 13.6 us -> 22.6 us
  starting transfers between devices: 16 us -> 22.5 us
  matrix products: 22.5 us -> 19.8 us
    ppermute x0 -> x3, waiting for transfers between devices: none -> 50.7 us  [doubled_up(): lax.ppermute(line, axis, [(d, (d - have) % ways) for d in range(ways)])]
    all_gather x1 -> x0, waiting for transfers between devices: 23.4 us -> none  [per_device(): lax.all_gather(cross_keyvalue_weight, 'seq', axis=0, tiled=True)]
    unnamed x19 -> x35, local copies, waits for them, and re-layouts: 2.45 us -> 10.2 us
    ppermute x0 -> x3, starting transfers between devices: none -> 4.22 us  [doubled_up(): lax.ppermute(line, axis, [(d, (d - have) % ways) for d in range(ways)])]
    dot_general x1, matrix products: 4.89 us -> 2.11 us  [per_device(): jnp.einsum('ycmq,qyb->mycb', self_attention_weights, all_keyval[1].reshap...]
    concatenate x0 -> x1, local copies, waits for them, and re-layouts: none -> 2.62 us  [doubled_up(): return jnp.roll(line, here * turn, axis=dim)]
    ppermute x5, starting transfers between devices: 16 us -> 18.3 us  [passed_along(): return lax.ppermute(block, axis, route)]
    concatenate x1, other arithmetic: 2.08 us -> 0.07 us  [per_device(): image_all = jnp.concatenate([earlier_tile, image_key_value], axis=0)]
  transfers between devices with their start and end apart: 7 -> 9, of which waited for: 4 -> 5; matrix products, arithmetic and copies ran while one was open for 14% -> 17% of each run, Pallas kernels for 0% -> 0%
where the time goes in v1:
time: 169 us; the launch traced here: 168 us
  waiting for transfers between devices  68.7 us (41%)
  local copies, waits for them, and re-layouts  22.6 us (13%)
  starting transfers between devices  22.5 us (13%)
  other arithmetic  20.5 us (12%)
  matrix products  19.8 us (12%)
  between operations  13.7 us (8%)
    ppermute x3, waiting for transfers between devices, doubled_up(): lax.ppermute(line, axis, [(d, (d - have) % ways) for d in range(ways)])  50.7 us
    ppermute x5, starting transfers between devices, passed_along(): return lax.ppermute(block, axis, route)  18.3 us
    ppermute x5, waiting for transfers between devices, passed_along(): return lax.ppermute(block, axis, route)  17.9 us
    sub x2, other arithmetic, attend_heads(): return jax.nn.softmax(scores, axis=-1)  12.5 us
    unnamed x35, local copies, waits for them, and re-layouts  10.2 us
    dot_general x2, matrix products, attend_heads(): jnp.einsum('tgrd,kgd->grtk', query_rows, keys, preferred_element_type=jnp...  5.54 us
    ppermute x3, starting transfers between devices, doubled_up(): lax.ppermute(line, axis, [(d, (d - have) % ways) for d in range(ways)])  4.22 us
    convert_element_type x1, other arithmetic, per_device(): (self_output + gate_cols[None, :] * cross_output).astype(jnp.bfloat16)  3.46 us
  transfers between devices with their start and end apart: 9, of which 5 were waited for; matrix products, arithmetic and copies ran while one was open for 17% of the time, Pallas kernels for 0%

profile of v1, /device:TPU:8, one launch (start us, length us, event | category | flops | bytes accessed | tf_op | source)
XLA Modules:
  0.0 167.8 jit_solution(5102160903002249379)
XLA Ops:
  12.4 3.2 %fusion.45 = (f32[8,256]{1,0:T(8,128)S(1)}, f32[8,256,256]{1,2,0:T(8,128)}) fusion(bf16[256,8,80]{0,2,1:T(8,128)(2,1)S(1)} %bitcast.87, bf16[256,8,80]{0,2,1:T(8,128)(2,1)} %bitcast.86), kind=kOutput, calls=%fused_computation.84 | convolution fusion | flops 85459200 | bytes 2760704 | tf_op jit(solution)/shard_map/sub | solution.py:61
  15.5 1.9 %convolution_convert_fusion = bf16[8,256,80]{1,2,0:T(8,128)(2,1)S(1)} fusion(bf16[256,8,80]{0,2,1:T(8,128)(2,1)S(1)} %bitcast.88, f32[8,256,256]{1,2,0:T(8,128)} %get-tuple-element.19, f32[8,256]{1,0:T(8,128)S(1)} %get-tuple-element.18), kind=kOutput, calls=%fused_computation.31 | convolution fusion | flops 85098496 | bytes 2760704 | tf_op jit(solution)/shard_map/hqk,khd->qhd/dot_general | solution.py:62
  19.3 2.5 %collective-permute-start.2 = (s32[128]{0:T(128)S(1)}, s32[128]{0:T(128)S(1)}, u32[]{:S(2)}, u32[]{:S(2)}) collective-permute-start(s32[128]{0:T(128)S(1)} %copy-done.8), channel_id=1, source_target_pairs={{0,2},{2,4},{4,6},{6,8},{8,10},{10,12},{12,14},{1,3},{3,5},{5,7},{... | collective-permute-start | bytes 1544 | tf_op jit(solution)/shard_map/ppermute | solution.py:27
  22.0 4.3 %collective-permute-start = (bf16[2,128,512]{1,2,0:T(8,128)(2,1)S(1)}, bf16[2,128,512]{1,2,0:T(8,128)(2,1)S(1)}, u32[]{:S(2)}, u32[]{:S(2)}) collective-permute-start(bf16[2,128,512]{1,2,0:T(8,128)(2,1)S(1)} %copy.28), channel_id=1, source_target_pairs={{0,2},{2,4},{4,6},{6,8},{8,10},{10,12},{12,14},{1,3},{3,5},{5,7},{... | collective-permute-start | bytes 786440 | tf_op jit(solution)/shard_map/ppermute | solution.py:27
  27.9 2.5 %collective-permute-start.3 = (s32[128]{0:T(128)S(1)}, s32[128]{0:T(128)S(1)}, u32[]{:S(2)}, u32[]{:S(2)}) collective-permute-start(s32[128]{0:T(128)S(1)} %collective-permute-done.2), channel_id=1, source_target_pairs={{0,2},{2,4},{4,6},{6,8},{8,10},{10,12},{12,14},{1,3},{3,5},{5,7},{... | collective-permute-start | bytes 1544 | tf_op jit(solution)/shard_map/ppermute | solution.py:27
  31.9 2.3 %collective-permute-done.3 = s32[128]{0:T(128)S(1)} collective-permute-done((s32[128]{0:T(128)S(1)}, s32[128]{0:T(128)S(1)}, u32[]{:S(2)}, u32[]{:S(2)}) %collective-permute-start.3) | collective-permute-done | bytes 544 | tf_op jit(solution)/shard_map/ppermute | solution.py:27
  34.2 2.0 %collective-permute-start.1 = (bf16[2,128,512]{1,2,0:T(8,128)(2,1)S(1)}, bf16[2,128,512]{1,2,0:T(8,128)(2,1)S(1)}, u32[]{:S(2)}, u32[]{:S(2)}) collective-permute-start(bf16[2,128,512]{1,2,0:T(8,128)(2,1)S(1)} %collective-permute-done), channel_id=1, source_target_pairs={{0,2},{2,4},{4,6},{6,8},{8,10},{10,12},{12,14},{1,3},{3,5},{5,7},{... | collective-permute-start | bytes 786440 | tf_op jit(solution)/shard_map/ppermute | solution.py:27
  37.8 8.5 %collective-permute-done.1 = bf16[2,128,512]{1,2,0:T(8,128)(2,1)S(1)} collective-permute-done((bf16[2,128,512]{1,2,0:T(8,128)(2,1)S(1)}, bf16[2,128,512]{1,2,0:T(8,128)(2,1)S(1)}, u32[]{:S(2)}, u32[]{:S(2)}) %collective-permute-start.1) | collective-permute-done | bytes 262176 | tf_op jit(solution)/shard_map/ppermute | solution.py:27
  47.2 4.2 %collective-permute-done.5 = bf16[320,2,512]{2,0,1:T(8,128)(2,1)S(1)} collective-permute-done((bf16[320,2,512]{2,0,1:T(8,128)(2,1)S(1)}, bf16[320,2,512]{2,0,1:T(8,128)(2,1)S(1)}, u32[]{:S(2)}, u32[]{:S(2)}) %collective-permute-start.5) | collective-permute-done | bytes 655392 | tf_op jit(solution)/shard_map/ppermute | solution.py:17
  52.6 2.3 %collective-permute-start.6 = (bf16[640,2,512]{2,0,1:T(8,128)(2,1)}, bf16[640,2,512]{2,0,1:T(8,128)(2,1)}, u32[]{:S(2)}, u32[]{:S(2)}) collective-permute-start(bf16[640,2,512]{2,0,1:T(8,128)(2,1)} %pad_maximum_fusion), channel_id=1, source_target_pairs={{0,8},{2,10},{4,12},{6,14},{8,0},{10,2},{12,4},{14,6},{1,9},{3,11}... | collective-permute-start | bytes 3932168 | tf_op jit(solution)/shard_map/ppermute | solution.py:17
  56.0 3.6 %fusion.44 = (f32[4,8,128]{2,1,0:T(8,128)S(1)}, f32[4,8,128,384]{2,3,1,0:T(8,128)}) fusion(f32[4,384,128,8]{2,1,3,0:T(8,128)S(1)} %fusion.22, pred[128,384]{0,1:T(8,128)(4,1)S(1)} %and_and_fusion), kind=kOutput, calls=%fused_computation.83 | output fusion | flops 9437567 | bytes 12648448 | tf_op jit(solution)/shard_map/sub | solution.py:35
  62.1 46.5 %collective-permute-done.6 = bf16[640,2,512]{2,0,1:T(8,128)(2,1)} collective-permute-done((bf16[640,2,512]{2,0,1:T(8,128)(2,1)}, bf16[640,2,512]{2,0,1:T(8,128)(2,1)}, u32[]{:S(2)}, u32[]{:S(2)}) %collective-permute-start.6) | collective-permute-done | bytes 1310752 | tf_op jit(solution)/shard_map/ppermute | solution.py:17
  108.6 2.5 %constant_dynamic-update-slice_fusion.4 = bf16[2560,2,512]{2,0,1:T(8,128)(2,1)} fusion(bf16[2560,2,512]{2,0,1:T(8,128)(2,1)} %constant_dynamic-update-slice_fusion.5, bf16[640,2,512]{2,0,1:T(8,128)(2,1)} %collective-permute-done.6), kind=kLoop, calls=%fused_computation.53 | loop fusion | bytes 2621440
  113.5 2.6 %constant_dynamic-update-slice_fusion = bf16[2560,2,512]{2,0,1:T(8,128)(2,1)} fusion(bf16[2560,2,512]{2,0,1:T(8,128)(2,1)} %constant_dynamic-update-slice_fusion.1, bf16[640,2,512]{2,0,1:T(8,128)(2,1)} %collective-permute-done.6), kind=kLoop, calls=%fused_computation.49 | loop fusion | bytes 2621440 | tf_op jit(solution)/shard_map/jit(_roll_dynamic)/concatenate | solution.py:21
  116.2 2.9 %fusion.16 = bf16[256,2,512]{2,0,1:T(8,128)(2,1)S(1)} fusion(bf16[2560,2,512]{2,0,1:T(8,128)(2,1)} %constant_dynamic-update-slice_fusion, s32[]{:T(128)S(6)} %select_n.32, f32[256,1280]{1,0:T(8,128)S(1)} %copy-done.2, bf16[256,1280]{1,0:T(8,128)(2,1)S(1)} %copy-done.3, f32[256]{0:T(256)S(1)} %add_rsqrt_fusion), kind=kOutput, calls=%fused_computation.30 | convolution fusion | flops 672661504 | bytes 5112836 | tf_op jit(solution)/shard_map/ic,cjf->ijf/dot_general | solution.py:71
  119.1 6.9 %collective-permute-start.7 = (bf16[256,2,512]{2,0,1:T(8,128)(2,1)S(1)}, bf16[256,2,512]{2,0,1:T(8,128)(2,1)S(1)}, u32[]{:S(2)}, u32[]{:S(2)}) collective-permute-start(bf16[256,2,512]{2,0,1:T(8,128)(2,1)S(1)} %fusion.16), channel_id=1, source_target_pairs={{0,2},{2,4},{4,6},{6,8},{8,10},{10,12},{12,14},{1,3},{3,5},{5,7},{... | collective-permute-start | bytes 1572872 | tf_op jit(solution)/shard_map/ppermute | solution.py:27
  126.0 2.1 %fusion.11 = f32[4,128,8,128]{3,1,2,0:T(8,128)} fusion(bf16[384,4,128,1]{0,2,3,1:T(8,128)(2,1)S(1)} %bitcast.84, f32[4,8,128,384]{2,3,1,0:T(8,128)S(1)} %copy-done.12, f32[4,8,128]{2,1,0:T(8,128)S(1)} %get-tuple-element.16), kind=kOutput, calls=%fused_computation.17 | convolution fusion | flops 405798912 | bytes 8798208 | tf_op jit(solution)/shard_map/ycmq,qyb->mycb/dot_general | solution.py:98
  128.1 2.9 %copy.47 = f32[128,4096]{1,0:T(8,128)} copy(f32[128,4096]{0,1:T(8,128)} %bitcast.80) | data formatting | bytes 4194304 | tf_op jit(solution)/shard_map/reshape | solution.py:104
  131.1 7.1 %collective-permute-done.7 = bf16[256,2,512]{2,0,1:T(8,128)(2,1)S(1)} collective-permute-done((bf16[256,2,512]{2,0,1:T(8,128)(2,1)S(1)}, bf16[256,2,512]{2,0,1:T(8,128)(2,1)S(1)}, u32[]{:S(2)}, u32[]{:S(2)}) %collective-permute-start.7) | collective-permute-done | bytes 524320 | tf_op jit(solution)/shard_map/ppermute | solution.py:27
  138.4 4.5 %fusion.20 = f32[4,512,128,8]{2,1,3,0:T(8,128)} fusion(bf16[128,4,8,128]{3,2,1,0:T(8,128)(2,1)S(1)} %bitcast.77, bf16[512,4,128,1]{2,1,0,3:T(4,128)(2,1)S(1)} %bitcast.78), kind=kOutput, calls=%fused_computation.35 | convolution fusion | flops 536870912 | bytes 9961472 | tf_op jit(solution)/shard_map/tgrd,kgd->grtk/dot_general | solution.py:31
  143.2 8.9 %fusion.46 = (f32[4,8,128]{2,1,0:T(8,128)S(1)}, f32[4,8,128,512]{2,3,1,0:T(8,128)S(1)}) fusion(f32[4,512,128,8]{2,1,3,0:T(8,128)} %fusion.20, pred[128,512]{0,1:T(8,128)(4,1)S(1)} %copy-done.7), kind=kOutput, calls=%fused_computation.85 | output fusion | flops 12583423 | bytes 16859136 | tf_op jit(solution)/shard_map/sub | solution.py:35
  152.1 2.3 %fusion.8 = f32[4,128,8,128]{3,1,2,0:T(8,128)} fusion(bf16[512,4,128,1]{0,2,3,1:T(8,128)(2,1)S(1)} %bitcast.83, f32[4,8,128,512]{2,3,1,0:T(8,128)S(1)} %get-tuple-element.21, f32[128]{0:T(128)S(1)} %copy-done.11, f32[4,8,128]{2,1,0:T(8,128)S(1)} %get-tuple-element.20), kind=kOutput, calls=%fused_computation.14 | convolution fusion | flops 543162368 | bytes 11026944 | tf_op jit(solution)/shard_map/ycmq,qyb->mycb/dot_general | solution.py:118
  154.4 3.1 %copy.46 = f32[128,4096]{1,0:T(8,128)} copy(f32[128,4096]{0,1:T(8,128)} %bitcast.79) | data formatting | bytes 4194304 | tf_op jit(solution)/shard_map/reshape | solution.py:124
  157.5 3.5 %add_convert_fusion = bf16[128,4096]{1,0:T(8,128)(2,1)} fusion(f32[128,4096]{1,0:T(8,128)} %copy.47, f32[128,4096]{1,0:T(8,128)} %copy.46, f32[4096]{0:T(1024)S(1)} %broadcast_bitcast_fusion), kind=kLoop, calls=%fused_computation.21 | loop fusion | flops 1572864 | bytes 5259264 | tf_op jit(solution)/shard_map/convert_element_type | solution.py:126
  (68 shorter events, 20.7 us)
Async XLA Ops:
  6.5 11.0 %copy-start = (bf16[640,1280]{1,0:T(8,128)(2,1)S(1)}, bf16[640,1280]{1,0:T(8,128)(2,1)}, u32[]{:S(2)}) copy-start(bf16[640,1280]{1,0:T(8,128)(2,1)} %param.15) | copy-start | bytes 4915204
  6.5 54.0 %all-reduce.2.cloned.1.call-start = ((), (), s32[]{:S(2)}) async-start(), calls=%async_computation | async-start | bytes 2621440 | tf_op jit(solution)/shard_map/psum | solution.py:67
  8.5 27.8 %collective-permute-start.4 = (bf16[160,2,512]{2,0,1:T(8,128)(2,1)S(1)}, bf16[160,2,512]{2,0,1:T(8,128)(2,1)S(1)}, u32[]{:S(2)}, u32[]{:S(2)}) collective-permute-start(bf16[160,2,512]{2,0,1:T(8,128)(2,1)S(1)} %get-tuple-element.12), channel_id=1, source_target_pairs={{0,14},{2,0},{4,2},{6,4},{8,6},{10,8},{12,10},{14,12},{1,15},{3,1}... | collective-permute-start | bytes 983048 | tf_op jit(solution)/shard_map/ppermute | solution.py:17
  15.5 3.8 %copy-start.8 = (s32[128]{0:T(128)S(1)}, s32[128]{0:T(128)}, u32[]{:S(2)}) copy-start(s32[128]{0:T(128)} %param.11) | copy-start | bytes 1540
  15.5 6.3 %copy-start.6 = (bf16[2,128,512]{2,1,0:T(8,128)(2,1)S(1)}, bf16[2,128,512]{2,1,0:T(8,128)(2,1)}, u32[]{:S(2)}) copy-start(bf16[2,128,512]{2,1,0:T(8,128)(2,1)} %param.10) | copy-start | bytes 786436
  17.5 8.9 %copy-start.9 = (s32[128,2]{0,1:T(2,128)S(1)}, s32[128,2]{0,1:T(2,128)}, u32[]{:S(2)}) copy-start(s32[128,2]{0,1:T(2,128)} %param.12) | copy-start | bytes 3076
  17.5 9.5 %copy-start.10 = (f32[32]{0:T(128)S(1)}, f32[32]{0:T(128)}, u32[]{:S(2)}) copy-start(f32[32]{0:T(128)} %param.17) | copy-start | bytes 388
  19.3 8.6 %collective-permute-start.2 = (s32[128]{0:T(128)S(1)}, s32[128]{0:T(128)S(1)}, u32[]{:S(2)}, u32[]{:S(2)}) collective-permute-start(s32[128]{0:T(128)S(1)} %copy-done.8), channel_id=1, source_target_pairs={{0,2},{2,4},{4,6},{6,8},{8,10},{10,12},{12,14},{1,3},{3,5},{5,7},{... | collective-permute-start | bytes 1544 | tf_op jit(solution)/shard_map/ppermute | solution.py:27
  22.0 12.2 %collective-permute-start = (bf16[2,128,512]{1,2,0:T(8,128)(2,1)S(1)}, bf16[2,128,512]{1,2,0:T(8,128)(2,1)S(1)}, u32[]{:S(2)}, u32[]{:S(2)}) collective-permute-start(bf16[2,128,512]{1,2,0:T(8,128)(2,1)S(1)} %copy.28), channel_id=1, source_target_pairs={{0,2},{2,4},{4,6},{6,8},{8,10},{10,12},{12,14},{1,3},{3,5},{5,7},{... | collective-permute-start | bytes 786440 | tf_op jit(solution)/shard_map/ppermute | solution.py:27
  27.9 6.3 %collective-permute-start.3 = (s32[128]{0:T(128)S(1)}, s32[128]{0:T(128)S(1)}, u32[]{:S(2)}, u32[]{:S(2)}) collective-permute-start(s32[128]{0:T(128)S(1)} %collective-permute-done.2), channel_id=1, source_target_pairs={{0,2},{2,4},{4,6},{6,8},{8,10},{10,12},{12,14},{1,3},{3,5},{5,7},{... | collective-permute-start | bytes 1544 | tf_op jit(solution)/shard_map/ppermute | solution.py:27
  34.2 12.0 %collective-permute-start.1 = (bf16[2,128,512]{1,2,0:T(8,128)(2,1)S(1)}, bf16[2,128,512]{1,2,0:T(8,128)(2,1)S(1)}, u32[]{:S(2)}, u32[]{:S(2)}) collective-permute-start(bf16[2,128,512]{1,2,0:T(8,128)(2,1)S(1)} %collective-permute-done), channel_id=1, source_target_pairs={{0,2},{2,4},{4,6},{6,8},{8,10},{10,12},{12,14},{1,3},{3,5},{5,7},{... | collective-permute-start | bytes 786440 | tf_op jit(solution)/shard_map/ppermute | solution.py:27
  36.3 15.1 %collective-permute-start.5 = (bf16[320,2,512]{2,0,1:T(8,128)(2,1)S(1)}, bf16[320,2,512]{2,0,1:T(8,128)(2,1)S(1)}, u32[]{:S(2)}, u32[]{:S(2)}) collective-permute-start(bf16[320,2,512]{2,0,1:T(8,128)(2,1)S(1)} %pad_maximum_fusion.2), channel_id=1, source_target_pairs={{0,12},{2,14},{4,0},{6,2},{8,4},{10,6},{12,8},{14,10},{1,13},{3,15... | collective-permute-start | bytes 1966088 | tf_op jit(solution)/shard_map/ppermute | solution.py:17
  52.6 56.0 %collective-permute-start.6 = (bf16[640,2,512]{2,0,1:T(8,128)(2,1)}, bf16[640,2,512]{2,0,1:T(8,128)(2,1)}, u32[]{:S(2)}, u32[]{:S(2)}) collective-permute-start(bf16[640,2,512]{2,0,1:T(8,128)(2,1)} %pad_maximum_fusion), channel_id=1, source_target_pairs={{0,8},{2,10},{4,12},{6,14},{8,0},{10,2},{12,4},{14,6},{1,9},{3,11}... | collective-permute-start | bytes 3932168 | tf_op jit(solution)/shard_map/ppermute | solution.py:17
  56.0 4.6 %copy-start.3 = (bf16[256,1280]{1,0:T(8,128)(2,1)S(1)}, bf16[256,1280]{1,0:T(8,128)(2,1)}, u32[]{:S(2)}) copy-start(bf16[256,1280]{1,0:T(8,128)(2,1)} %param.13) | copy-start | bytes 1966084
  59.6 51.5 %copy-start.4 = (bf16[160,2,512]{2,1,0:T(2,128)(2,1)S(1)}, bf16[160,2,512]{2,1,0:T(2,128)(2,1)}, u32[]{:S(2)}) copy-start(bf16[160,2,512]{2,1,0:T(2,128)(2,1)} %param.16) | copy-start | bytes 983044
  62.1 54.1 %copy-start.2 = (f32[256,1280]{1,0:T(8,128)S(1)}, f32[256,1280]{1,0:T(8,128)}, u32[]{:S(2)}) copy-start(f32[256,1280]{1,0:T(8,128)} %all-reduce.2.cloned.1.call-done) | copy-start | bytes 3932164
  113.5 12.5 %copy-start.5 = (bf16[1,384,512]{1,2,0:T(8,128)(2,1)S(1)}, bf16[1,384,512]{1,2,0:T(8,128)(2,1)}, u32[]{:S(2)}) copy-start(bf16[1,384,512]{1,2,0:T(8,128)(2,1)} %get-tuple-element.11) | copy-start | bytes 1179652
  113.5 12.5 %copy-start.12 = (f32[4,8,128,384]{2,3,1,0:T(8,128)S(1)}, f32[4,8,128,384]{2,3,1,0:T(8,128)}, u32[]{:S(2)}) copy-start(f32[4,8,128,384]{2,3,1,0:T(8,128)} %get-tuple-element.17) | copy-start | bytes 18874372
  119.1 19.1 %collective-permute-start.7 = (bf16[256,2,512]{2,0,1:T(8,128)(2,1)S(1)}, bf16[256,2,512]{2,0,1:T(8,128)(2,1)S(1)}, u32[]{:S(2)}, u32[]{:S(2)}) collective-permute-start(bf16[256,2,512]{2,0,1:T(8,128)(2,1)S(1)} %fusion.16), channel_id=1, source_target_pairs={{0,2},{2,4},{4,6},{6,8},{8,10},{10,12},{12,14},{1,3},{3,5},{5,7},{... | collective-permute-start | bytes 1572872 | tf_op jit(solution)/shard_map/ppermute | solution.py:27
  138.4 4.7 %copy-start.7 = (pred[128,512]{0,1:T(8,128)(4,1)S(1)}, pred[128,512]{0,1:T(8,128)(4,1)}, u32[]{:S(2)}) copy-start(pred[128,512]{0,1:T(8,128)(4,1)} %compare_and_fusion) | copy-start | bytes 196612
  143.2 8.9 %copy-start.11 = (f32[128]{0:T(128)S(1)}, f32[128]{0:T(128)}, u32[]{:S(2)}) copy-start(f32[128]{0:T(128)} %compare_convert_fusion) | copy-start | bytes 1540
  154.4 6.5 %copy-start.1 = (bf16[640,1280]{1,0:T(8,128)(2,1)S(1)}, bf16[640,1280]{1,0:T(8,128)(2,1)}, u32[]{:S(2)}) copy-start(bf16[640,1280]{1,0:T(8,128)(2,1)} %param.15) | copy-start | bytes 4915204
Sparse Core Ops, SparseCore 0:
  19.4 20.5 all-reduce.1
